TPU v7x, 32 devices: a whole 2x2x4 slice. The times are simulated.
32 devices in a mesh: groups: 1, wide: 32 (over z, y, x, core), narrow: 1.
Axes of the slice: x: 2, y: 2, z: 4, core: 2. Of those that a mesh axis runs over, the one named last changes fastest.
Arguments:
- gamma_tensor: bfloat16 [256, 128, 1024], P(('groups', 'wide'), None, 'narrow'), may hold values from -6 to 6
- three_center: bfloat16 [256, 128, 1024], P(('groups', 'wide'), None, 'narrow'), may hold values from -6 to 6
- gamma_blocks: int32 [256, 2, 16], P(('groups', 'wide'), None, 'narrow'), may hold values 0 or 1
- center_blocks: int32 [256, 2, 16], P(('groups', 'wide'), None, 'narrow'), may hold values 0 or 1
Outputs:
- density_occ: float32 [128, 128], P(('groups', 'wide', 'narrow'))
- gamma_aux: float32 [256, 256], P(('groups', 'wide', 'narrow'))
All inputs are finite; a program needn't handle non-finite values. No bound on the sum of `gamma_blocks` or of `center_blocks` on one device may be relied on, other than what follows from the above.
Results may differ from a plain program's by a relative error of at most 0.0003.
Values may be sent and summed in bfloat16 or wider, within the bound.
A program may use at most 64 MiB of HBM per device.

v0:
```python
import math

import jax
import jax.numpy as jnp
from jax import lax
from jax.sharding import PartitionSpec as P

BLK = 64


def apply_blocks(tensor, block_mask):
    aux_rows, occ_cols, vir_cols = tensor.shape
    shaped = tensor.reshape(aux_rows, occ_cols // BLK, BLK, vir_cols // BLK, BLK)
    factor = block_mask.astype(tensor.dtype)[:, :, None, :, None]
    return (shaped * factor).reshape(aux_rows, occ_cols, vir_cols)


def spread_sum(row_term, total_rows):
    wide_count = lax.axis_size("wide")
    narrow_count = lax.axis_size("narrow")
    own_rows = total_rows // (wide_count * narrow_count)
    full_term = row_term(0, total_rows)
    columns = full_term.shape[1]
    shaped = full_term.reshape(wide_count, narrow_count, own_rows, columns)
    halved = lax.psum_scatter(shaped, "narrow", scatter_dimension=1, tiled=True)
    summed = lax.psum_scatter(halved, "wide", scatter_dimension=0, tiled=True)
    result = summed.reshape(own_rows, columns)
    return result


def local(gamma_tensor, three_center, gamma_blocks, center_blocks):
    wide_count = lax.axis_size("wide")
    narrow_count = lax.axis_size("narrow")
    gamma_local = apply_blocks(gamma_tensor, gamma_blocks)
    center_local = apply_blocks(three_center, center_blocks)
    total_aux = gamma_tensor.shape[0] * wide_count
    total_occ = gamma_tensor.shape[1]
    total_vir = gamma_tensor.shape[2] * narrow_count
    occ_scale = -1.0 / math.sqrt(total_aux * total_vir)
    aux_scale = 1.0 / math.sqrt(total_occ * total_vir)

    def occ_term(first_row, row_count):
        product = lax.dot_general(
            gamma_local,
            center_local,
            (((0, 2), (0, 2)), ((), ())),
            preferred_element_type=jnp.float32,
        )
        return product * occ_scale

    density_occ = spread_sum(occ_term, total_occ)
    moved_pair = (
        lax.all_to_all(gamma_local, "wide", split_axis=1, concat_axis=0, tiled=True),
        lax.all_to_all(center_local, "wide", split_axis=1, concat_axis=0, tiled=True),
    )
    gamma_occ, center_occ = moved_pair

    def aux_term(first_row, row_count):
        product = lax.dot_general(
            gamma_occ, center_occ, (((1, 2), (1, 2)), ((), ())), preferred_element_type=jnp.float32
        )
        return product * aux_scale

    gamma_aux = spread_sum(aux_term, total_aux)
    return (density_occ, gamma_aux)


def solution(mesh):
    in_specs = (
        P(("groups", "wide"), None, "narrow"),
        P(("groups", "wide"), None, "narrow"),
        P(("groups", "wide"), None, "narrow"),
        P(("groups", "wide"), None, "narrow"),
    )
    out_specs = (P(("groups", "wide", "narrow"), None), P(("groups", "wide", "narrow"), None))
    return jax.shard_map(local, mesh=mesh, in_specs=in_specs, out_specs=out_specs, check_vma=False)
```

profile of v0, /device:TPU:0, one launch (start us, length us, event | category | flops | bytes accessed | tf_op | source)
XLA Modules:
  0.0 370.0 jit_solution(17639156155540038429)
XLA Ops:
  7.2 0.7 convert_element_type.7
  7.9 3.1 mul.37
  10.9 0.0 copy-start.2
  10.9 5.5 %mul.38 = bf16[8,128,1024]{2,0,1:T(8,128)(2,1)S(1)} reshape(bf16[8,2,64,16,64]{4,3,0,2,1:T(8,128)(2,1)} %mul.37) | data formatting | bytes 4194304 | tf_op jit(solution)/shard_map/mul | solution.py:15
  16.4 0.0 copy-done.2
  16.5 3.1 mul.34
  19.5 6.5 %mul.35 = bf16[8,128,1024]{2,0,1:T(8,128)(2,1)} reshape(bf16[8,2,64,16,64]{4,3,0,2,1:T(8,128)(2,1)} %mul.34) | data formatting | bytes 4194304 | tf_op jit(solution)/shard_map/mul | solution.py:15
  26.1 6.7 %copy_multiply_fusion = (bf16[8,128,1024]{2,0,1:T(8,128)(2,1)S(1)}, bf16[8,128,1024]{2,0,1:T(8,128)(2,1)}) fusion(bf16[8,128,1024]{2,0,1:T(8,128)(2,1)S(1)} %mul.38, bf16[8,128,1024]{2,1,0:T(8,128)(2,1)} %param.5, bf16[8,128,1024]{2,0,1:T(8,128)(2,1)} %mul.35, bf16[8,128,1024]{2,1,0:T(8,128)(2,1)} %param.4), kind=kLoop, calls=%fused_computation.8 | loop fusion | flops 2097152 | bytes 12582912 | tf_op jit(solution)/shard_map/mul | solution.py:15
  32.8 0.0 copy-start
  32.8 55.9 %all_to_all.36 = bf16[8,128,1024]{2,0,1:T(8,128)(2,1)} all-to-all(bf16[8,128,1024]{2,0,1:T(8,128)(2,1)S(1)} %get-tuple-element.2), channel_id=1, replica_groups=mesh['groups'=1,'wide'=32,'narrow'=1] {'wide'}, dimensions={1} | all-to-all | bytes 4194304 | tf_op jit(solution)/shard_map/all_to_all | solution.py:54
  88.7 0.0 copy-done
  88.7 0.0 copy-start.1
  88.7 3.8 %all-to-all-start = ((bf16[8,128,1024]{2,0,1:T(8,128)(2,1)}), bf16[8,128,1024]{2,0,1:T(8,128)(2,1)}, u32[]{:S(2)}, u32[]{:S(2)}) async-start(bf16[8,128,1024]{2,0,1:T(8,128)(2,1)} %get-tuple-element.3), calls=%async_computation | async-start | bytes 4194304 | tf_op jit(solution)/shard_map/all_to_all | solution.py:53
  92.5 0.0 all-reduce.3.cloned.1.call-start
  92.5 0.0 copy-done.1
  92.5 6.7 %fusion.28 = f32[128,128]{1,0:T(8,128)} fusion(bf16[8,128,1024]{2,0,1:T(8,128)(2,1)S(1)} %copy-done.1, bf16[8,128,1024]{2,0,1:T(8,128)(2,1)} %get-tuple-element.3), kind=kOutput, calls=%fused_computation.14 | convolution fusion | flops 268451840 | bytes 4259840 | tf_op jit(solution)/shard_map/dot_general | solution.py:43
  99.2 0.0 all-reduce.3.cloned.1.call-update
  99.2 0.0 reduce-scatter.2.cloned.1.call-start
  99.3 42.7 %all-to-all-done = bf16[8,128,1024]{2,0,1:T(8,128)(2,1)} async-done(((bf16[8,128,1024]{2,0,1:T(8,128)(2,1)}), bf16[8,128,1024]{2,0,1:T(8,128)(2,1)}, u32[]{:S(2)}, u32[]{:S(2)}) %all-to-all-start) | async-done | bytes 2097184 | tf_op jit(solution)/shard_map/all_to_all | solution.py:53
  142.0 3.7 fusion.18
  145.6 0.0 reduce-scatter.2.cloned.1.call-update
  145.7 80.0 %all-reduce.3.cloned.1.call-done = f32[32,1,4,128]{3,2,1,0:T(4,128)} async-done(((f32[32,1,4,128]{3,2,1,0:T(4,128)}), f32[32,1,4,128]{3,2,1,0:T(4,128)}) %all-reduce.3.cloned.1.call-update) | async-done | bytes 65552
  225.7 1.3 dynamic-slice_bitcast_fusion
  227.0 136.2 %reduce-scatter.2.cloned.1.call-done = f32[1,1,8,256]{3,2,1,0:T(8,128)} async-done(((f32[32,1,8,256]{3,2,1,0:T(8,128)}), f32[1,1,8,256]{3,2,1,0:T(8,128)}) %reduce-scatter.2.cloned.1.call-update) | async-done | bytes 8208 | tf_op jit(solution)/shard_map/reduce_scatter | solution.py:26
  (3 shorter events, 0.0 us)
Async XLA Ops:
  10.9 5.5 %copy-start.2 = (s32[8,2,16]{2,1,0:T(2,128)S(1)}, s32[8,2,16]{2,1,0:T(2,128)}, u32[]{:S(2)}) copy-start(s32[8,2,16]{2,1,0:T(2,128)} %param.6) | copy-start | bytes 3076
  32.8 55.9 %copy-start = (bf16[8,128,1024]{2,0,1:T(8,128)(2,1)}, bf16[8,128,1024]{2,0,1:T(8,128)(2,1)S(1)}, u32[]{:S(2)}) copy-start(bf16[8,128,1024]{2,0,1:T(8,128)(2,1)S(1)} %get-tuple-element.2) | copy-start | bytes 6291460
  88.7 3.9 %copy-start.1 = (bf16[8,128,1024]{2,0,1:T(8,128)(2,1)S(1)}, bf16[8,128,1024]{2,0,1:T(8,128)(2,1)}, u32[]{:S(2)}) copy-start(bf16[8,128,1024]{2,0,1:T(8,128)(2,1)} %copy-done) | copy-start | bytes 6291460
  88.7 53.3 %all-to-all-start = ((bf16[8,128,1024]{2,0,1:T(8,128)(2,1)}), bf16[8,128,1024]{2,0,1:T(8,128)(2,1)}, u32[]{:S(2)}, u32[]{:S(2)}) async-start(bf16[8,128,1024]{2,0,1:T(8,128)(2,1)} %get-tuple-element.3), calls=%async_computation | async-start | bytes 4194304 | tf_op jit(solution)/shard_map/all_to_all | solution.py:53
  92.5 133.2 %all-reduce.3.cloned.1.call-start = ((), (), s32[]{:S(2)}) async-start(), calls=%async_computation.4 | async-start | bytes 131072
  99.2 263.9 %reduce-scatter.2.cloned.1.call-start = ((), (), s32[]{:S(2)}) async-start(), calls=%async_computation.3 | async-start | bytes 270336 | tf_op jit(solution)/shard_map/reduce_scatter | solution.py:26
Sparse Core Ops, SparseCore 0:
  99.3 126.3 all-reduce.2
  228.5 134.5 reduce-scatter.1
where the time goes:
time: 370 us
  waiting for transfers between devices  259 us (70%)
  blocking collectives  55.9 us (15%)
  local copies, waits for them, and re-layouts  19.4 us (5%)
  between operations  14.1 us (4%)
  matrix products  10.3 us (3%)
  other arithmetic  7.41 us (2%)
  starting transfers between devices  3.88 us (1%)
    reduce_scatter x1, waiting for transfers between devices, spread_sum(): summed = lax.psum_scatter(halved, 'wide', scatter_dimension=0, tiled=True)  136 us
    unnamed x3, waiting for transfers between devices  80.1 us
    all_to_all x1, blocking collectives, local(): lax.all_to_all(center_local, 'wide', split_axis=1, concat_axis=0, tiled=T...  55.9 us
    all_to_all x1, waiting for transfers between devices, local(): lax.all_to_all(gamma_local, 'wide', split_axis=1, concat_axis=0, tiled=True)  42.7 us
    mul x4, local copies, waits for them, and re-layouts, apply_blocks(): return (shaped * factor).reshape(aux_rows, occ_cols, vir_cols)  18.1 us
  transfers between devices with their start and end apart: 3, of which 3 were waited for; matrix products, arithmetic and copies ran while one was open for 3% of the time, Pallas kernels for 0%

commit v1 on v0

--- a/solution.py
+++ b/solution.py
@@ -21,10 +21,11 @@
     own_rows = total_rows // (wide_count * narrow_count)
     full_term = row_term(0, total_rows)
     columns = full_term.shape[1]
-    shaped = full_term.reshape(wide_count, narrow_count, own_rows, columns)
-    halved = lax.psum_scatter(shaped, "narrow", scatter_dimension=1, tiled=True)
-    summed = lax.psum_scatter(halved, "wide", scatter_dimension=0, tiled=True)
-    result = summed.reshape(own_rows, columns)
+    shaped = full_term.reshape(wide_count, narrow_count * own_rows, columns)
+    parts = lax.all_to_all(shaped, "wide", split_axis=0, concat_axis=0, tiled=True)
+    result = jnp.sum(parts, axis=0)
+    if narrow_count > 1:
+        result = lax.psum_scatter(result, "narrow", scatter_dimension=0, tiled=True)
     return result
 
 

time: 370 us -> 161 us (0.44)
  waiting for transfers between devices: 259 us -> 55.9 us
  between operations: 14.1 us -> 0.7 us
  starting transfers between devices: 3.88 us -> 10.4 us
    reduce_scatter x1 -> x0, waiting for transfers between devices: 136 us -> none  [spread_sum(): summed = lax.psum_scatter(halved, 'wide', scatter_dimension=0, tiled=True)]
    unnamed x3 -> x0, waiting for transfers between devices: 80.1 us -> none
    all_to_all x0 -> x2, waiting for transfers between devices: none -> 13.7 us  [spread_sum(): lax.all_to_all(shaped, 'wide', split_axis=0, concat_axis=0, tiled=True)]
    all_to_all x0 -> x2, starting transfers between devices: none -> 6.59 us  [spread_sum(): lax.all_to_all(shaped, 'wide', split_axis=0, concat_axis=0, tiled=True)]
  transfers between devices with their start and end apart: 3 -> 3, of which waited for: 3 -> 3; matrix products, arithmetic and copies ran while one was open for 3% -> 7% of each run, Pallas kernels for 0% -> 0%
where the time goes in v1:
time: 161 us; the launch traced here: 160 us
  blocking collectives  55.9 us (35%)
  waiting for transfers between devices  55.9 us (35%)
  local copies, waits for them, and re-layouts  18.1 us (11%)
  starting transfers between devices  10.4 us (6%)
  matrix products  10.3 us (6%)
  other arithmetic  8.66 us (5%)
    all_to_all x1, blocking collectives, local(): lax.all_to_all(center_local, 'wide', split_axis=1, concat_axis=0, tiled=T...  55.9 us
    all_to_all x1, waiting for transfers between devices, local(): lax.all_to_all(gamma_local, 'wide', split_axis=1, concat_axis=0, tiled=True)  42.2 us
    mul x4, local copies, waits for them, and re-layouts, apply_blocks(): return (shaped * factor).reshape(aux_rows, occ_cols, vir_cols)  18.1 us
    all_to_all x2, waiting for transfers between devices, spread_sum(): lax.all_to_all(shaped, 'wide', split_axis=0, concat_axis=0, tiled=True)  13.7 us
    mul x1, other arithmetic, apply_blocks(): return (shaped * factor).reshape(aux_rows, occ_cols, vir_cols)  6.7 us
    dot_general x1, matrix products, occ_term(): lax.dot_general(gamma_local, center_local, (((0, 2), (0, 2)), ((), ())),...  6.68 us
    all_to_all x2, starting transfers between devices, spread_sum(): lax.all_to_all(shaped, 'wide', split_axis=0, concat_axis=0, tiled=True)  6.59 us
    all_to_all x1, starting transfers between devices, local(): lax.all_to_all(gamma_local, 'wide', split_axis=1, concat_axis=0, tiled=True)  3.8 us
  transfers between devices with their start and end apart: 3, of which 3 were waited for; matrix products, arithmetic and copies ran while one was open for 7% of the time, Pallas kernels for 0%

profile of v1, /device:TPU:0, one launch (start us, length us, event | category | flops | bytes accessed | tf_op | source)
XLA Modules:
  0.0 160.0 jit_solution(1777910200095321613)
XLA Ops:
  0.6 0.7 convert_element_type.7
  1.3 3.0 %mul.37 = bf16[8,2,64,16,64]{4,3,0,2,1:T(8,128)(2,1)} broadcast(bf16[8,2,16]{2,0,1:T(8,128)(2,1)S(1)} %copy.10), dimensions={0,1,3} | broadcast | bytes 2097664 | tf_op jit(solution)/shard_map/mul | solution.py:15
  4.4 0.0 copy-start.2
  4.4 5.5 %mul.38 = bf16[8,128,1024]{2,0,1:T(8,128)(2,1)S(1)} reshape(bf16[8,2,64,16,64]{4,3,0,2,1:T(8,128)(2,1)} %mul.37) | data formatting | bytes 4194304 | tf_op jit(solution)/shard_map/mul | solution.py:15
  9.9 0.0 copy-done.2
  9.9 3.0 %mul.34 = bf16[8,2,64,16,64]{4,3,0,2,1:T(8,128)(2,1)} broadcast(bf16[8,2,16]{2,0,1:T(8,128)(2,1)S(1)} %copy.8), dimensions={0,1,3} | broadcast | bytes 2097664 | tf_op jit(solution)/shard_map/mul | solution.py:15
  13.0 6.5 %mul.35 = bf16[8,128,1024]{2,0,1:T(8,128)(2,1)} reshape(bf16[8,2,64,16,64]{4,3,0,2,1:T(8,128)(2,1)} %mul.34) | data formatting | bytes 4194304 | tf_op jit(solution)/shard_map/mul | solution.py:15
  19.5 6.7 %copy_multiply_fusion = (bf16[8,128,1024]{2,0,1:T(8,128)(2,1)S(1)}, bf16[8,128,1024]{2,0,1:T(8,128)(2,1)}) fusion(bf16[8,128,1024]{2,0,1:T(8,128)(2,1)S(1)} %mul.38, bf16[8,128,1024]{2,1,0:T(8,128)(2,1)} %param.5, bf16[8,128,1024]{2,0,1:T(8,128)(2,1)} %mul.35, bf16[8,128,1024]{2,1,0:T(8,128)(2,1)} %param.4), kind=kLoop, calls=%fused_computation.8 | loop fusion | flops 2097152 | bytes 12582912 | tf_op jit(solution)/shard_map/mul | solution.py:15
  26.2 0.0 copy-start
  26.2 55.9 %all_to_all.46 = bf16[8,128,1024]{2,0,1:T(8,128)(2,1)} all-to-all(bf16[8,128,1024]{2,0,1:T(8,128)(2,1)S(1)} %get-tuple-element.2), channel_id=1, replica_groups=mesh['groups'=1,'wide'=32,'narrow'=1] {'wide'}, dimensions={1} | all-to-all | bytes 4194304 | tf_op jit(solution)/shard_map/all_to_all | solution.py:55
  82.1 0.0 copy-done
  82.1 0.0 copy-start.1
  82.1 3.8 %all-to-all-start.1 = ((bf16[8,128,1024]{2,0,1:T(8,128)(2,1)}), bf16[8,128,1024]{2,0,1:T(8,128)(2,1)}, u32[]{:S(2)}, u32[]{:S(2)}) async-start(bf16[8,128,1024]{2,0,1:T(8,128)(2,1)} %get-tuple-element.3), calls=%async_computation.1 | async-start | bytes 4194304 | tf_op jit(solution)/shard_map/all_to_all | solution.py:54
  85.9 0.0 copy-done.1
  85.9 6.7 %fusion.28 = f32[128,128]{1,0:T(8,128)} fusion(bf16[8,128,1024]{2,0,1:T(8,128)(2,1)S(1)} %copy-done.1, bf16[8,128,1024]{2,0,1:T(8,128)(2,1)} %get-tuple-element.3), kind=kOutput, calls=%fused_computation.14 | convolution fusion | flops 268451840 | bytes 4259840 | tf_op jit(solution)/shard_map/dot_general | solution.py:44
  92.6 42.2 %all-to-all-done.1 = bf16[8,128,1024]{2,0,1:T(8,128)(2,1)} async-done(((bf16[8,128,1024]{2,0,1:T(8,128)(2,1)}), bf16[8,128,1024]{2,0,1:T(8,128)(2,1)}, u32[]{:S(2)}, u32[]{:S(2)}) %all-to-all-start.1) | async-done | bytes 2097184 | tf_op jit(solution)/shard_map/all_to_all | solution.py:54
  134.8 4.0 %all-to-all-start = ((f32[32,4,128]{2,1,0:T(4,128)}), f32[32,4,128]{2,1,0:T(4,128)S(1)}, u32[]{:S(2)}, u32[]{:S(2)}) async-start(f32[32,4,128]{2,1,0:T(4,128)} %bitcast.1), calls=%async_computation | async-start | bytes 131072 | tf_op jit(solution)/shard_map/all_to_all | solution.py:25
  138.8 3.7 %fusion.18 = f32[32,8,256]{2,1,0:T(8,128)} fusion(bf16[8,32,4,1024]{3,0,2,1:T(8,128)(2,1)} %bitcast.45, bf16[8,32,4,1024]{3,0,2,1:T(8,128)(2,1)} %bitcast.2), kind=kOutput, calls=%fused_computation.12 | convolution fusion | flops 536936448 | bytes 4456448 | tf_op jit(solution)/shard_map/dot_general | solution.py:60
  142.5 3.7 %all-to-all-done = f32[32,4,128]{2,1,0:T(4,128)S(1)} async-done(((f32[32,4,128]{2,1,0:T(4,128)}), f32[32,4,128]{2,1,0:T(4,128)S(1)}, u32[]{:S(2)}, u32[]{:S(2)}) %all-to-all-start) | async-done | bytes 65568 | tf_op jit(solution)/shard_map/all_to_all | solution.py:25
  146.2 2.6 %all-to-all-start.3 = ((f32[32,8,256]{2,1,0:T(8,128)}), f32[32,8,256]{2,1,0:T(8,128)S(1)}, u32[]{:S(2)}, u32[]{:S(2)}) async-start(f32[32,8,256]{2,1,0:T(8,128)} %fusion.18), calls=%async_computation.3 | async-start | bytes 524288 | tf_op jit(solution)/shard_map/all_to_all | solution.py:25
  148.8 0.6 reduce_sum.18
  149.4 10.0 %all-to-all-done.3 = f32[32,8,256]{2,1,0:T(8,128)S(1)} async-done(((f32[32,8,256]{2,1,0:T(8,128)}), f32[32,8,256]{2,1,0:T(8,128)S(1)}, u32[]{:S(2)}, u32[]{:S(2)}) %all-to-all-start.3) | async-done | bytes 262176 | tf_op jit(solution)/shard_map/all_to_all | solution.py:25
  159.4 0.6 reduce_sum.19
  (3 shorter events, 0.0 us)
Async XLA Ops:
  4.4 5.5 %copy-start.2 = (s32[8,2,16]{2,1,0:T(2,128)S(1)}, s32[8,2,16]{2,1,0:T(2,128)}, u32[]{:S(2)}) copy-start(s32[8,2,16]{2,1,0:T(2,128)} %param.6) | copy-start | bytes 3076
  26.2 55.9 %copy-start = (bf16[8,128,1024]{2,0,1:T(8,128)(2,1)}, bf16[8,128,1024]{2,0,1:T(8,128)(2,1)S(1)}, u32[]{:S(2)}) copy-start(bf16[8,128,1024]{2,0,1:T(8,128)(2,1)S(1)} %get-tuple-element.2) | copy-start | bytes 6291460
  82.1 3.8 %copy-start.1 = (bf16[8,128,1024]{2,0,1:T(8,128)(2,1)S(1)}, bf16[8,128,1024]{2,0,1:T(8,128)(2,1)}, u32[]{:S(2)}) copy-start(bf16[8,128,1024]{2,0,1:T(8,128)(2,1)} %copy-done) | copy-start | bytes 6291460
  82.1 52.7 %all-to-all-start.1 = ((bf16[8,128,1024]{2,0,1:T(8,128)(2,1)}), bf16[8,128,1024]{2,0,1:T(8,128)(2,1)}, u32[]{:S(2)}, u32[]{:S(2)}) async-start(bf16[8,128,1024]{2,0,1:T(8,128)(2,1)} %get-tuple-element.3), calls=%async_computation.1 | async-start | bytes 4194304 | tf_op jit(solution)/shard_map/all_to_all | solution.py:54
  134.8 11.4 %all-to-all-start = ((f32[32,4,128]{2,1,0:T(4,128)}), f32[32,4,128]{2,1,0:T(4,128)S(1)}, u32[]{:S(2)}, u32[]{:S(2)}) async-start(f32[32,4,128]{2,1,0:T(4,128)} %bitcast.1), calls=%async_computation | async-start | bytes 131072 | tf_op jit(solution)/shard_map/all_to_all | solution.py:25
  146.2 13.2 %all-to-all-start.3 = ((f32[32,8,256]{2,1,0:T(8,128)}), f32[32,8,256]{2,1,0:T(8,128)S(1)}, u32[]{:S(2)}, u32[]{:S(2)}) async-start(f32[32,8,256]{2,1,0:T(8,128)} %fusion.18), calls=%async_computation.3 | async-start | bytes 524288 | tf_op jit(solution)/shard_map/all_to_all | solution.py:25

commit v2 on v0

v2 whole, which is shorter than its diff:
```python
import functools
import math

import jax
import jax.numpy as jnp
from jax import lax
from jax.experimental import pallas as pl
from jax.experimental.pallas import tpu as pltpu
from jax.sharding import PartitionSpec as P

BLK = 64
ROWS = 16
LANES = 128
MESH = pl.DeviceIdType.MESH
F32 = jnp.float32
BF16 = jnp.bfloat16
NT = (((1,), (1,)), ((), ()))


def kernel(
    n, occ_scale, aux_scale,
    g_ref, c_ref, gb_ref, cb_ref, occ_ref, aux_ref,
    mask, keep, stage, send, recv, gram, occ_part, occ_recv, aux_part, aux_recv,
    send_sem, recv_sem, occ_send_sem, occ_recv_sem, aux_send_sem, aux_recv_sem,
):
    me = lax.axis_index("wide")
    aux, occ, vir = g_ref.shape
    blocks = occ // BLK
    row_parts = occ // ROWS
    lane_parts = n // row_parts
    width = vir // lane_parts
    own_occ = occ // n

    def partner(step):
        half = (step + 1) // 2
        sign = 1 - 2 * (step % 2)
        return lax.rem(me + n // 2 + sign * half + n, n)

    barrier = pltpu.get_barrier_semaphore()

    @pl.loop(0, n - 1)
    def _(step):
        pl.semaphore_signal(barrier, inc=1, device_id={"wide": partner(step)}, device_id_type=MESH)

    spread = (
        lax.broadcasted_iota(jnp.int32, (vir // BLK, vir), 1) // BLK
        == lax.broadcasted_iota(jnp.int32, (vir // BLK, vir), 0)
    ).astype(F32)
    for t, b_ref in enumerate((gb_ref, cb_ref)):
        for p in range(aux):
            lines = jnp.dot(b_ref[p].astype(F32), spread, preferred_element_type=F32)
            for b in range(blocks):
                mask[t, p, b] = jnp.broadcast_to(lines[b : b + 1], (8, vir))

    def prepare(dest, out):
        row = pl.multiple_of((dest // lane_parts) * ROWS, ROWS)
        block = (dest // lane_parts) * ROWS // BLK
        for w in range(width // LANES):
            lane = pl.multiple_of((dest % lane_parts) * width + w * LANES, LANES)
            for t, src in enumerate((g_ref, c_ref)):
                for p in range(aux):
                    x = src[p, pl.ds(row, ROWS), pl.ds(lane, LANES)].astype(F32)
                    m = mask[t, p, block, :, pl.ds(lane, LANES)]
                    y = x * jnp.concatenate([m] * (ROWS // 8), axis=0)
                    keep[t, p, pl.ds(row, ROWS), pl.ds(lane, LANES)] = y.astype(BF16)
                    stage[w, pl.ds(t * aux + p, ROWS, stride=2 * aux), :] = y
            for i in range(ROWS):
                piece = stage[w, i * 2 * aux : (i + 1) * 2 * aux, :]
                at = i * width + w * LANES
                out[:, at : at + LANES] = piece.astype(BF16)

    def moved(peer, slot):
        return pltpu.make_async_remote_copy(
            src_ref=send.at[peer], dst_ref=recv.at[slot], send_sem=send_sem.at[peer],
            recv_sem=recv_sem.at[slot], device_id={"wide": peer}, device_id_type=MESH)

    def occ_moved(peer, slot):
        return pltpu.make_async_remote_copy(
            src_ref=occ_part.at[peer], dst_ref=occ_recv.at[slot], send_sem=occ_send_sem.at[peer],
            recv_sem=occ_recv_sem.at[slot], device_id={"wide": peer}, device_id_type=MESH)

    def aux_moved(peer, slot):
        return pltpu.make_async_remote_copy(
            src_ref=aux_part.at[peer], dst_ref=aux_recv.at[slot], send_sem=aux_send_sem.at[peer],
            recv_sem=aux_recv_sem.at[slot], device_id={"wide": peer}, device_id_type=MESH)

    pl.semaphore_wait(barrier, n - 1)

    @pl.loop(0, n - 1)
    def _(step):
        dest = partner(step)
        prepare(dest, send.at[dest])
        moved(dest, me).start()

    prepare(me, recv.at[me])

    def occ_step(p, total):
        return total + lax.dot_general(keep[0, p], keep[1, p], NT, preferred_element_type=F32)

    total = lax.fori_loop(0, aux, occ_step, jnp.zeros((occ, occ), F32)) * occ_scale
    for d in range(n):
        occ_part[d] = total[d * own_occ : (d + 1) * own_occ]
    occ_recv[me] = occ_part[me]

    @pl.loop(0, n - 1)
    def _(step):
        occ_moved(partner(step), me).start()

    @pl.loop(0, n - 1)
    def _(step):
        peer = partner(step)
        moved(peer, peer).wait_recv()

    depth = ROWS * width
    cut = depth // 4
    rows = n * 2 * aux
    gram[...] = jnp.zeros_like(gram)

    @pl.loop(0, depth // cut)
    def _(k):
        x = recv[:, :, pl.ds(pl.multiple_of(k * cut, LANES), cut)].reshape(rows, cut)
        gram[...] += lax.dot_general(x, x, NT, preferred_element_type=F32)

    product = gram[...].reshape(n, 2 * aux, rows)[:, :aux].reshape(n * aux, rows)
    r = lax.broadcasted_iota(jnp.int32, (rows, n * aux), 0)
    q = lax.broadcasted_iota(jnp.int32, (rows, n * aux), 1)
    pick = (r == (q // aux) * (2 * aux) + aux + q % aux).astype(F32)
    picked = jnp.dot(product, pick, precision=lax.Precision.HIGHEST, preferred_element_type=F32)
    aux_part[...] = (picked * aux_scale).reshape(n, aux, n * aux)
    aux_recv[me] = aux_part[me]

    @pl.loop(0, n - 1)
    def _(step):
        aux_moved(partner(step), me).start()

    @pl.loop(0, n - 1)
    def _(step):
        peer = partner(step)
        occ_moved(peer, peer).wait_recv()

    occ_ref[...] = jnp.sum(occ_recv[...], axis=0)

    @pl.loop(0, n - 1)
    def _(step):
        peer = partner(step)
        moved(peer, peer).wait_send()
        occ_moved(peer, peer).wait_send()

    @pl.loop(0, n - 1)
    def _(step):
        peer = partner(step)
        aux_moved(peer, peer).wait_recv()

    aux_ref[...] = jnp.sum(aux_recv[...], axis=0)

    @pl.loop(0, n - 1)
    def _(step):
        peer = partner(step)
        aux_moved(peer, peer).wait_send()


def local(gamma_tensor, three_center, gamma_blocks, center_blocks):
    n = lax.axis_size("wide")
    narrow = lax.axis_size("narrow")
    aux, occ, vir = gamma_tensor.shape
    occ_scale = -1.0 / math.sqrt(aux * n * vir * narrow)
    aux_scale = 1.0 / math.sqrt(occ * vir * narrow)
    width = vir // (n // (occ // ROWS))
    rows = n * 2 * aux
    dma = pltpu.SemaphoreType.DMA((n,))
    density_occ, gamma_aux = pl.pallas_call(
        functools.partial(kernel, n, occ_scale, aux_scale),
        out_shape=(
            jax.ShapeDtypeStruct((occ // n, occ), F32),
            jax.ShapeDtypeStruct((aux, n * aux), F32),
        ),
        in_specs=[pl.BlockSpec(memory_space=pltpu.VMEM)] * 4,
        out_specs=(pl.BlockSpec(memory_space=pltpu.VMEM),) * 2,
        scratch_shapes=[
            pltpu.VMEM((2, aux, occ // BLK, 8, vir), F32),
            pltpu.VMEM((2, aux, occ, vir), BF16),
            pltpu.VMEM((width // LANES, ROWS * 2 * aux, LANES), F32),
            pltpu.VMEM((n, 2 * aux, ROWS * width), BF16),
            pltpu.VMEM((n, 2 * aux, ROWS * width), BF16),
            pltpu.VMEM((rows, rows), F32),
            pltpu.VMEM((n, occ // n, occ), F32),
            pltpu.VMEM((n, occ // n, occ), F32),
            pltpu.VMEM((n, aux, n * aux), F32),
            pltpu.VMEM((n, aux, n * aux), F32),
            dma, dma, dma, dma, dma, dma,
        ],
        compiler_params=pltpu.CompilerParams(
            collective_id=0, has_side_effects=True, vmem_limit_bytes=56 * 1024 * 1024
        ),
    )(gamma_tensor, three_center, gamma_blocks, center_blocks)
    if narrow > 1:
        density_occ = lax.psum_scatter(density_occ, "narrow", scatter_dimension=0, tiled=True)
        gamma_aux = lax.psum_scatter(gamma_aux, "narrow", scatter_dimension=0, tiled=True)
    return (density_occ, gamma_aux)


def solution(mesh):
    spread = P(("groups", "wide"), None, "narrow")
    out = P(("groups", "wide", "narrow"), None)
    return jax.shard_map(
        local, mesh=mesh, in_specs=(spread,) * 4, out_specs=(out, out), check_vma=False
    )
```

time: 370 us -> 129 us (0.35)
  waiting for transfers between devices: 259 us -> 0 us
  Pallas kernels: 0 us -> 125 us
  blocking collectives: 55.9 us -> 0 us
  local copies, waits for them, and re-layouts: 19.4 us -> 2.53 us
  between operations: 14.1 us -> 0.64 us
  matrix products: 10.3 us -> 0 us
  other arithmetic: 7.41 us -> 0 us
  starting transfers between devices: 3.88 us -> 0 us
    reduce_scatter x1 -> x0, waiting for transfers between devices: 136 us -> none  [spread_sum(): summed = lax.psum_scatter(halved, 'wide', scatter_dimension=0, tiled=True)]
    pallas_call x0 -> x1, Pallas kernels: none -> 125 us  [local(): pl.pallas_call(functools.partial(kernel, n, occ_scale, aux_scale), out_sh...]
    unnamed x3 -> x0, waiting for transfers between devices: 80.1 us -> none
    all_to_all x1 -> x0, blocking collectives: 55.9 us -> none  [local(): lax.all_to_all(center_local, 'wide', split_axis=1, concat_axis=0, tiled=T...]
    all_to_all x1 -> x0, waiting for transfers between devices: 42.7 us -> none  [local(): lax.all_to_all(gamma_local, 'wide', split_axis=1, concat_axis=0, tiled=True)]
    mul x4 -> x0, local copies, waits for them, and re-layouts: 18.1 us -> none  [apply_blocks(): return (shaped * factor).reshape(aux_rows, occ_cols, vir_cols)]
    dot_general x2 -> x0, matrix products: 10.3 us -> none  [the longest x1 6.67 us: occ_term(): lax.dot_general(gamma_local, center_local, (((0, 2), (0, 2)), ((), ())),...]
    mul x1 -> x0, other arithmetic: 6.7 us -> none  [apply_blocks(): return (shaped * factor).reshape(aux_rows, occ_cols, vir_cols)]
  transfers between devices with their start and end apart: 3 -> 0, of which waited for: 3 -> 0; matrix products, arithmetic and copies ran while one was open for 3% -> 0% of each run, Pallas kernels for 0% -> 0%
where the time goes in v2:
time: 129 us; the launch traced here: 128 us
  Pallas kernels  125 us (97%)
  local copies, waits for them, and re-layouts  2.53 us (2%)
    pallas_call x1, Pallas kernels, local(): pl.pallas_call(functools.partial(kernel, n, occ_scale, aux_scale), out_sh...  125 us

profile of v2, /device:TPU:0, one launch (start us, length us, event | category | flops | bytes accessed | tf_op | source)
XLA Modules:
  0.0 128.3 jit_solution(823775170111006322)
XLA Ops:
  0.6 125.1 %shard_map.59 = (f32[4,128]{1,0:T(4,128)}, f32[8,256]{1,0:T(8,128)}) custom-call(bf16[8,128,1024]{2,1,0:T(8,128)(2,1)} %g_ref.1, bf16[8,128,1024]{2,1,0:T(8,128)(2,1)} %c_ref.1, s32[8,2,16]{2,1,0:T(2,128)} %gb_ref.1, s32[8,2,16]{2,1,0:T(2,128)} %cb_ref.1), custom_call_target="tpu_custom_call" | custom-call | tf_op jit(solution)/shard_map/pallas_call | solution.py:171
  125.8 1.2 copy.8
  127.0 1.3 %copy.9 = f32[8,256]{1,0:T(8,128)} copy(f32[8,256]{1,0:T(8,128)} %get-tuple-element.5) | data formatting | bytes 16384

commit v3 on v2

v3 whole, which is shorter than its diff:
```python
import functools
import math

import jax
import jax.numpy as jnp
from jax import lax
from jax.experimental import pallas as pl
from jax.experimental.pallas import tpu as pltpu
from jax.sharding import PartitionSpec as P

BLK = 64
ROWS = 16
LANES = 128
MESH = pl.DeviceIdType.MESH
F32 = jnp.float32
BF16 = jnp.bfloat16
NT = (((1,), (1,)), ((), ()))


def kernel(
    n, occ_scale, aux_scale,
    g_hbm, c_hbm, gb_ref, cb_ref, occ_ref, aux_ref,
    g_ref, c_ref, mask, keep, stage, send, recv, g_all, c_all,
    occ_part, occ_recv, occ_mid, occ_far, aux_part, aux_recv, aux_mid, aux_far,
    load_sem, send_sem, recv_sem, occ_send_sem, occ_recv_sem, aux_send_sem, aux_recv_sem, far_sem,
):
    me = lax.axis_index("wide")
    aux, occ, vir = g_ref.shape
    blocks = occ // BLK
    row_parts = occ // ROWS
    lane_parts = n // row_parts
    width = vir // lane_parts
    own_occ = occ // n
    half = n // 2
    side = lax.div(me, half)
    place = lax.rem(me, half)
    mirror = (1 - side) * half + place

    def flip(index, step, bits):
        peer = 0
        for b in range(bits):
            both = lax.div(index, 1 << b) + lax.div(step, 1 << (bits - 1 - b))
            peer += lax.rem(both, 2) * (1 << b)
        return peer

    def partner(step):
        return flip(me, step, n.bit_length() - 1)

    def neighbour(step):
        return flip(place, step, half.bit_length() - 1)

    loads = [
        pltpu.make_async_copy(g_hbm, g_ref, load_sem.at[0]),
        pltpu.make_async_copy(c_hbm, c_ref, load_sem.at[1]),
    ]
    for load in loads:
        load.start()

    barrier = pltpu.get_barrier_semaphore()

    @pl.loop(1, n)
    def _(step):
        pl.semaphore_signal(barrier, inc=1, device_id={"wide": partner(step)}, device_id_type=MESH)

    spread = (
        lax.broadcasted_iota(jnp.int32, (vir // BLK, vir), 1) // BLK
        == lax.broadcasted_iota(jnp.int32, (vir // BLK, vir), 0)
    ).astype(F32)
    for t, b_ref in enumerate((gb_ref, cb_ref)):
        for p in range(aux):
            lines = jnp.dot(b_ref[p].astype(F32), spread, preferred_element_type=F32)
            for b in range(blocks):
                mask[t, p, b] = jnp.broadcast_to(lines[b : b + 1], (8, vir))

    def prepare(dest, out):
        row = pl.multiple_of((dest // lane_parts) * ROWS, ROWS)
        block = (dest // lane_parts) * ROWS // BLK
        for w in range(width // LANES):
            lane = pl.multiple_of((dest % lane_parts) * width + w * LANES, LANES)
            for t, src in enumerate((g_ref, c_ref)):
                for p in range(aux):
                    x = src[p, pl.ds(row, ROWS), pl.ds(lane, LANES)].astype(F32)
                    m = mask[t, p, block, :, pl.ds(lane, LANES)]
                    y = x * jnp.concatenate([m] * (ROWS // 8), axis=0)
                    keep[t, p, pl.ds(row, ROWS), pl.ds(lane, LANES)] = y.astype(BF16)
                    stage[w, pl.ds(t * aux + p, ROWS, stride=2 * aux), :] = y
            for i in range(ROWS):
                piece = stage[w, i * 2 * aux : (i + 1) * 2 * aux, :]
                at = i * width + w * LANES
                out[:, at : at + LANES] = piece.astype(BF16)

    def moved(peer, slot):
        return pltpu.make_async_remote_copy(
            src_ref=send.at[peer], dst_ref=recv.at[slot], send_sem=send_sem.at[peer],
            recv_sem=recv_sem.at[slot], device_id={"wide": peer}, device_id_type=MESH)

    def summed(part, received, sems):
        def one(peer, slot):
            return pltpu.make_async_remote_copy(
                src_ref=part.at[peer], dst_ref=received.at[slot], send_sem=sems[0].at[peer],
                recv_sem=sems[1].at[slot], device_id={"wide": side * half + peer},
                device_id_type=MESH)
        return one

    def across(mid, far, slot):
        return pltpu.make_async_remote_copy(
            src_ref=mid.at[1 - side], dst_ref=far, send_sem=far_sem.at[slot],
            recv_sem=far_sem.at[slot + 1], device_id={"wide": mirror}, device_id_type=MESH)

    occ_moved = summed(occ_part, occ_recv, (occ_send_sem, occ_recv_sem))
    aux_moved = summed(aux_part, aux_recv, (aux_send_sem, aux_recv_sem))
    occ_across = across(occ_mid, occ_far, 0)
    aux_across = across(aux_mid, aux_far, 2)

    for load in loads:
        load.wait()
    first = partner(1)
    prepare(first, send.at[first])
    pl.semaphore_wait(barrier, n - 1)
    moved(first, me).start()

    @pl.loop(2, n)
    def _(step):
        dest = partner(step)
        prepare(dest, send.at[dest])
        moved(dest, me).start()

    prepare(me, recv.at[me])

    def occ_step(p, total):
        return total + lax.dot_general(keep[0, p], keep[1, p], NT, preferred_element_type=F32)

    total = lax.fori_loop(0, aux, occ_step, jnp.zeros((occ, occ), F32)) * occ_scale
    for d in range(n):
        occ_part[d % half, d // half] = total[d * own_occ : (d + 1) * own_occ]
    occ_recv[place] = occ_part[place]

    @pl.loop(1, half)
    def _(step):
        occ_moved(neighbour(step), place).start()

    @pl.loop(1, half)
    def _(step):
        peer = partner(step)
        moved(peer, peer).wait_recv()

    depth = ROWS * width

    @pl.loop(half, n)
    def _(step):
        peer = partner(step)
        moved(peer, peer).wait_recv()
        pair = lax.div(peer, 2)
        for k in range(0, depth, 512):
            x = recv[2 * pair, :, k : k + 512].astype(F32)
            y = recv[2 * pair + 1, :, k : k + 512].astype(F32)
            g_all[pair, :, k : k + 512] = jnp.concatenate([x[:aux], y[:aux]], axis=0).astype(BF16)
            c_all[pair, :, k : k + 512] = jnp.concatenate([x[aux:], y[aux:]], axis=0).astype(BF16)

    product = lax.dot_general(
        g_all[...].reshape(n * aux, depth), c_all[...].reshape(n * aux, depth), NT,
        preferred_element_type=F32,
    )
    spread_rows = (product * aux_scale).reshape(2, half, aux, n * aux)
    for h in range(2):
        aux_part[:, h] = spread_rows[h]

    @pl.loop(1, half)
    def _(step):
        aux_moved(neighbour(step), place).start()

    aux_recv[place] = aux_part[place]

    @pl.loop(1, half)
    def _(step):
        peer = neighbour(step)
        occ_moved(peer, peer).wait_recv()

    occ_mid[...] = jnp.sum(occ_recv[...], axis=0)
    occ_across.start()

    @pl.loop(1, n)
    def _(step):
        peer = partner(step)
        moved(peer, peer).wait_send()

    @pl.loop(1, half)
    def _(step):
        peer = neighbour(step)
        occ_moved(peer, peer).wait_send()

    @pl.loop(1, half)
    def _(step):
        peer = neighbour(step)
        aux_moved(peer, peer).wait_recv()

    aux_mid[...] = jnp.sum(aux_recv[...], axis=0)
    aux_across.start()

    @pl.loop(1, half)
    def _(step):
        peer = neighbour(step)
        aux_moved(peer, peer).wait_send()

    occ_across.wait()
    occ_ref[...] = occ_mid[side] + occ_far[...]
    aux_across.wait()
    aux_ref[...] = aux_mid[side] + aux_far[...]


def local(gamma_tensor, three_center, gamma_blocks, center_blocks):
    n = lax.axis_size("wide")
    narrow = lax.axis_size("narrow")
    aux, occ, vir = gamma_tensor.shape
    occ_scale = -1.0 / math.sqrt(aux * n * vir * narrow)
    aux_scale = 1.0 / math.sqrt(occ * vir * narrow)
    width = vir // (n // (occ // ROWS))
    half = n // 2
    own_occ = occ // n
    part_dma = pltpu.SemaphoreType.DMA((half,))
    dma = pltpu.SemaphoreType.DMA((n,))
    density_occ, gamma_aux = pl.pallas_call(
        functools.partial(kernel, n, occ_scale, aux_scale),
        out_shape=(
            jax.ShapeDtypeStruct((occ // n, occ), F32),
            jax.ShapeDtypeStruct((aux, n * aux), F32),
        ),
        in_specs=[pl.BlockSpec(memory_space=pl.ANY)] * 2
        + [pl.BlockSpec(memory_space=pltpu.VMEM)] * 2,
        out_specs=(pl.BlockSpec(memory_space=pltpu.VMEM),) * 2,
        scratch_shapes=[
            pltpu.VMEM((aux, occ, vir), BF16),
            pltpu.VMEM((aux, occ, vir), BF16),
            pltpu.VMEM((2, aux, occ // BLK, 8, vir), F32),
            pltpu.VMEM((2, aux, occ, vir), BF16),
            pltpu.VMEM((width // LANES, ROWS * 2 * aux, LANES), F32),
            pltpu.VMEM((n, 2 * aux, ROWS * width), BF16),
            pltpu.VMEM((n, 2 * aux, ROWS * width), BF16),
            pltpu.VMEM((half, 2 * aux, ROWS * width), BF16),
            pltpu.VMEM((half, 2 * aux, ROWS * width), BF16),
            pltpu.VMEM((half, 2, own_occ, occ), F32),
            pltpu.VMEM((half, 2, own_occ, occ), F32),
            pltpu.VMEM((2, own_occ, occ), F32),
            pltpu.VMEM((own_occ, occ), F32),
            pltpu.VMEM((half, 2, aux, n * aux), F32),
            pltpu.VMEM((half, 2, aux, n * aux), F32),
            pltpu.VMEM((2, aux, n * aux), F32),
            pltpu.VMEM((aux, n * aux), F32),
            pltpu.SemaphoreType.DMA((2,)),
            dma, dma, part_dma, part_dma, part_dma, part_dma,
            pltpu.SemaphoreType.DMA((4,)),
        ],
        compiler_params=pltpu.CompilerParams(
            collective_id=0, has_side_effects=True, vmem_limit_bytes=56 * 1024 * 1024
        ),
    )(gamma_tensor, three_center, gamma_blocks, center_blocks)
    if narrow > 1:
        density_occ = lax.psum_scatter(density_occ, "narrow", scatter_dimension=0, tiled=True)
        gamma_aux = lax.psum_scatter(gamma_aux, "narrow", scatter_dimension=0, tiled=True)
    return (density_occ, gamma_aux)


def solution(mesh):
    spread = P(("groups", "wide"), None, "narrow")
    out = P(("groups", "wide", "narrow"), None)
    return jax.shard_map(
        local, mesh=mesh, in_specs=(spread,) * 4, out_specs=(out, out), check_vma=False
    )
```

time: 129 us -> 117 us (0.907)
  Pallas kernels: 125 us -> 113 us
    pallas_call x1, Pallas kernels: 125 us -> 113 us  [local(): pl.pallas_call(functools.partial(kernel, n, occ_scale, aux_scale), out_sh...]
where the time goes in v3:
time: 117 us; the launch traced here: 116 us
  Pallas kernels  113 us (97%)
  local copies, waits for them, and re-layouts  2.53 us (2%)
    pallas_call x1, Pallas kernels, local(): pl.pallas_call(functools.partial(kernel, n, occ_scale, aux_scale), out_sh...  113 us
    unnamed x2, local copies, waits for them, and re-layouts  2.53 us

profile of v3, /device:TPU:0, one launch (start us, length us, event | category | flops | bytes accessed | tf_op | source)
XLA Modules:
  0.0 116.3 jit_solution(17334025010979856465)
XLA Ops:
  0.6 113.1 %shard_map.59 = (f32[4,128]{1,0:T(4,128)}, f32[8,256]{1,0:T(8,128)}) custom-call(bf16[8,128,1024]{2,1,0:T(8,128)(2,1)} %g_hbm.1, bf16[8,128,1024]{2,1,0:T(8,128)(2,1)} %c_hbm.1, s32[8,2,16]{2,1,0:T(2,128)} %gb_ref.1, s32[8,2,16]{2,1,0:T(2,128)} %cb_ref.1), custom_call_target="tpu_custom_call" | custom-call | tf_op jit(solution)/shard_map/pallas_call | solution.py:222
  113.7 1.2 %copy.8 = f32[4,128]{1,0:T(4,128)} copy(f32[4,128]{1,0:T(4,128)} %get-tuple-element.4) | data formatting | bytes 4096
  115.0 1.3 %copy.9 = f32[8,256]{1,0:T(8,128)} copy(f32[8,256]{1,0:T(8,128)} %get-tuple-element.5) | data formatting | bytes 16384

commit v4 on v3

--- a/solution.py
+++ b/solution.py
@@ -22,7 +22,7 @@
     g_hbm, c_hbm, gb_ref, cb_ref, occ_ref, aux_ref,
     g_ref, c_ref, mask, keep, stage, send, recv, g_all, c_all,
     occ_part, occ_recv, occ_mid, occ_far, aux_part, aux_recv, aux_mid, aux_far,
-    load_sem, send_sem, recv_sem, occ_send_sem, occ_recv_sem, aux_send_sem, aux_recv_sem, far_sem,
+    load_sem, send_sem, recv_sem, occ_sem, aux_sem, far_sem,
 ):
     me = lax.axis_index("wide")
     aux, occ, vir = g_ref.shape
@@ -89,43 +89,47 @@
                 at = i * width + w * LANES
                 out[:, at : at + LANES] = piece.astype(BF16)
 
-    def moved(peer, slot):
+    def moved(peer, step):
         return pltpu.make_async_remote_copy(
-            src_ref=send.at[peer], dst_ref=recv.at[slot], send_sem=send_sem.at[peer],
-            recv_sem=recv_sem.at[slot], device_id={"wide": peer}, device_id_type=MESH)
-
-    def summed(part, received, sems):
-        def one(peer, slot):
-            return pltpu.make_async_remote_copy(
-                src_ref=part.at[peer], dst_ref=received.at[slot], send_sem=sems[0].at[peer],
-                recv_sem=sems[1].at[slot], device_id={"wide": side * half + peer},
-                device_id_type=MESH)
-        return one
+            src_ref=send.at[step], dst_ref=recv.at[step], send_sem=send_sem.at[0],
+            recv_sem=recv_sem.at[step], device_id={"wide": peer}, device_id_type=MESH)
+
+    def take(buffer, sem):
+        pltpu.make_async_copy(buffer, buffer, sem).wait()
+
+    def exchange(part, received, sems):
+        @pl.loop(1, half)
+        def _(step):
+            peer = neighbour(step)
+            pltpu.make_async_remote_copy(
+                src_ref=part.at[peer], dst_ref=received.at[step], send_sem=sems.at[0],
+                recv_sem=sems.at[1], device_id={"wide": side * half + peer},
+                device_id_type=MESH).start()
+
+        received[0] = part[place]
 
     def across(mid, far, slot):
         return pltpu.make_async_remote_copy(
             src_ref=mid.at[1 - side], dst_ref=far, send_sem=far_sem.at[slot],
             recv_sem=far_sem.at[slot + 1], device_id={"wide": mirror}, device_id_type=MESH)
 
-    occ_moved = summed(occ_part, occ_recv, (occ_send_sem, occ_recv_sem))
-    aux_moved = summed(aux_part, aux_recv, (aux_send_sem, aux_recv_sem))
     occ_across = across(occ_mid, occ_far, 0)
     aux_across = across(aux_mid, aux_far, 2)
 
     for load in loads:
         load.wait()
     first = partner(1)
-    prepare(first, send.at[first])
+    prepare(first, send.at[1])
     pl.semaphore_wait(barrier, n - 1)
-    moved(first, me).start()
+    moved(first, 1).start()
 
     @pl.loop(2, n)
     def _(step):
         dest = partner(step)
-        prepare(dest, send.at[dest])
-        moved(dest, me).start()
-
-    prepare(me, recv.at[me])
+        prepare(dest, send.at[step])
+        moved(dest, step).start()
+
+    prepare(me, recv.at[0])
 
     def occ_step(p, total):
         return total + lax.dot_general(keep[0, p], keep[1, p], NT, preferred_element_type=F32)
@@ -133,27 +137,24 @@
     total = lax.fori_loop(0, aux, occ_step, jnp.zeros((occ, occ), F32)) * occ_scale
     for d in range(n):
         occ_part[d % half, d // half] = total[d * own_occ : (d + 1) * own_occ]
-    occ_recv[place] = occ_part[place]
+    exchange(occ_part, occ_recv, occ_sem)
 
     @pl.loop(1, half)
     def _(step):
-        occ_moved(neighbour(step), place).start()
-
-    @pl.loop(1, half)
-    def _(step):
-        peer = partner(step)
-        moved(peer, peer).wait_recv()
+        take(recv.at[step], recv_sem.at[step])
 
     depth = ROWS * width
+    odd = lax.rem(me, 2)
 
     @pl.loop(half, n)
     def _(step):
-        peer = partner(step)
-        moved(peer, peer).wait_recv()
-        pair = lax.div(peer, 2)
+        take(recv.at[step], recv_sem.at[step])
+        pair = lax.div(partner(step), 2)
+        even_slot = step - half + half * odd
+        odd_slot = step - half * odd
         for k in range(0, depth, 512):
-            x = recv[2 * pair, :, k : k + 512].astype(F32)
-            y = recv[2 * pair + 1, :, k : k + 512].astype(F32)
+            x = recv[even_slot, :, k : k + 512].astype(F32)
+            y = recv[odd_slot, :, k : k + 512].astype(F32)
             g_all[pair, :, k : k + 512] = jnp.concatenate([x[:aux], y[:aux]], axis=0).astype(BF16)
             c_all[pair, :, k : k + 512] = jnp.concatenate([x[aux:], y[aux:]], axis=0).astype(BF16)
 
@@ -165,47 +166,26 @@
     for h in range(2):
         aux_part[:, h] = spread_rows[h]
 
-    @pl.loop(1, half)
-    def _(step):
-        aux_moved(neighbour(step), place).start()
-
-    aux_recv[place] = aux_part[place]
-
-    @pl.loop(1, half)
-    def _(step):
-        peer = neighbour(step)
-        occ_moved(peer, peer).wait_recv()
-
+    exchange(aux_part, aux_recv, aux_sem)
+    others = pl.ds(1, half - 1)
+    take(occ_recv.at[others], occ_sem.at[1])
     occ_mid[...] = jnp.sum(occ_recv[...], axis=0)
     occ_across.start()
-
-    @pl.loop(1, n)
-    def _(step):
-        peer = partner(step)
-        moved(peer, peer).wait_send()
-
-    @pl.loop(1, half)
-    def _(step):
-        peer = neighbour(step)
-        occ_moved(peer, peer).wait_send()
-
-    @pl.loop(1, half)
-    def _(step):
-        peer = neighbour(step)
-        aux_moved(peer, peer).wait_recv()
-
+    take(send.at[pl.ds(1, n - 1)], send_sem.at[0])
+    take(occ_recv.at[others], occ_sem.at[0])
+    take(aux_recv.at[others], aux_sem.at[1])
     aux_mid[...] = jnp.sum(aux_recv[...], axis=0)
     aux_across.start()
-
-    @pl.loop(1, half)
-    def _(step):
-        peer = neighbour(step)
-        aux_moved(peer, peer).wait_send()
-
+    take(aux_recv.at[others], aux_sem.at[0])
     occ_across.wait()
     occ_ref[...] = occ_mid[side] + occ_far[...]
     aux_across.wait()
     aux_ref[...] = aux_mid[side] + aux_far[...]
+
+
+def hand_over(occ_in, aux_in, occ_out, aux_out):
+    occ_out[...] = occ_in[...]
+    aux_out[...] = aux_in[...]
 
 
 def local(gamma_tensor, three_center, gamma_blocks, center_blocks):
@@ -217,8 +197,6 @@
     width = vir // (n // (occ // ROWS))
     half = n // 2
     own_occ = occ // n
-    part_dma = pltpu.SemaphoreType.DMA((half,))
-    dma = pltpu.SemaphoreType.DMA((n,))
     density_occ, gamma_aux = pl.pallas_call(
         functools.partial(kernel, n, occ_scale, aux_scale),
         out_shape=(
@@ -247,7 +225,10 @@
             pltpu.VMEM((2, aux, n * aux), F32),
             pltpu.VMEM((aux, n * aux), F32),
             pltpu.SemaphoreType.DMA((2,)),
-            dma, dma, part_dma, part_dma, part_dma, part_dma,
+            pltpu.SemaphoreType.DMA((1,)),
+            pltpu.SemaphoreType.DMA((n,)),
+            pltpu.SemaphoreType.DMA((2,)),
+            pltpu.SemaphoreType.DMA((2,)),
             pltpu.SemaphoreType.DMA((4,)),
         ],
         compiler_params=pltpu.CompilerParams(
@@ -257,6 +238,16 @@
     if narrow > 1:
         density_occ = lax.psum_scatter(density_occ, "narrow", scatter_dimension=0, tiled=True)
         gamma_aux = lax.psum_scatter(gamma_aux, "narrow", scatter_dimension=0, tiled=True)
+    else:
+        density_occ, gamma_aux = pl.pallas_call(
+            hand_over,
+            out_shape=(
+                jax.ShapeDtypeStruct(density_occ.shape, F32),
+                jax.ShapeDtypeStruct(gamma_aux.shape, F32),
+            ),
+            in_specs=[pl.BlockSpec(memory_space=pltpu.VMEM)] * 2,
+            out_specs=(pl.BlockSpec(memory_space=pltpu.VMEM),) * 2,
+        )(density_occ, gamma_aux)
     return (density_occ, gamma_aux)
 
 

time: 117 us -> 114 us (0.974)
  local copies, waits for them, and re-layouts: 2.53 us -> 0 us
    unnamed x2 -> x0, local copies, waits for them, and re-layouts: 2.53 us -> none
    pallas_call x0 -> x1, Pallas kernels: none -> 1.31 us  [local(): pl.pallas_call(hand_over, out_shape=(jax.ShapeDtypeStruct(density_occ.sha...]
where the time goes in v4:
time: 114 us
  Pallas kernels  113 us (99%)
    pallas_call x1, Pallas kernels, local(): pl.pallas_call(functools.partial(kernel, n, occ_scale, aux_scale), out_sh...  112 us

profile of v4, /device:TPU:0, one launch (start us, length us, event | category | flops | bytes accessed | tf_op | source)
XLA Modules:
  0.0 114.0 jit_solution(7618218416117910746)
XLA Ops:
  0.6 112.1 %shard_map.59 = (f32[4,128]{1,0:T(4,128)}, f32[8,256]{1,0:T(8,128)}) custom-call(bf16[8,128,1024]{2,1,0:T(8,128)(2,1)} %g_hbm.1, bf16[8,128,1024]{2,1,0:T(8,128)(2,1)} %c_hbm.1, s32[8,2,16]{2,1,0:T(2,128)} %gb_ref.1, s32[8,2,16]{2,1,0:T(2,128)} %cb_ref.1), custom_call_target="tpu_custom_call" | custom-call | tf_op jit(solution)/shard_map/pallas_call | solution.py:200
  112.7 1.3 %shard_map.60 = (f32[4,128]{1,0:T(4,128)}, f32[8,256]{1,0:T(8,128)}) custom-call(f32[4,128]{1,0:T(4,128)} %get-tuple-element.4.occ_in, f32[8,256]{1,0:T(8,128)} %get-tuple-element.5.aux_in), custom_call_target="tpu_custom_call" | custom-call | tf_op jit(solution)/shard_map/pallas_call | solution.py:242

commit v5 on v4

--- a/solution.py
+++ b/solution.py
@@ -11,6 +11,7 @@
 BLK = 64
 ROWS = 16
 LANES = 128
+SIDES = 16
 MESH = pl.DeviceIdType.MESH
 F32 = jnp.float32
 BF16 = jnp.bfloat16
@@ -18,11 +19,11 @@
 
 
 def kernel(
-    n, occ_scale, aux_scale,
+    n, sides, occ_scale, aux_scale,
     g_hbm, c_hbm, gb_ref, cb_ref, occ_ref, aux_ref,
     g_ref, c_ref, mask, keep, stage, send, recv, g_all, c_all,
     occ_part, occ_recv, occ_mid, occ_far, aux_part, aux_recv, aux_mid, aux_far,
-    load_sem, send_sem, recv_sem, occ_sem, aux_sem, far_sem,
+    load_sem, send_sem, recv_sem, occ_sem, aux_sem, occ_far_sem, aux_far_sem,
 ):
     me = lax.axis_index("wide")
     aux, occ, vir = g_ref.shape
@@ -32,9 +33,9 @@
     width = vir // lane_parts
     own_occ = occ // n
     half = n // 2
-    side = lax.div(me, half)
-    place = lax.rem(me, half)
-    mirror = (1 - side) * half + place
+    group = n // sides
+    side = lax.div(me, group)
+    place = lax.rem(me, group)
 
     def flip(index, step, bits):
         peer = 0
@@ -47,21 +48,22 @@
         return flip(me, step, n.bit_length() - 1)
 
     def neighbour(step):
-        return flip(place, step, half.bit_length() - 1)
+        return flip(place, step, group.bit_length() - 1)
 
     loads = [
         pltpu.make_async_copy(g_hbm, g_ref, load_sem.at[0]),
         pltpu.make_async_copy(c_hbm, c_ref, load_sem.at[1]),
     ]
+
+    barrier = pltpu.get_barrier_semaphore()
+
+    @pl.loop(1, n)
+    def _(step):
+        peer = lax.rem(me + step, n)
+        pl.semaphore_signal(barrier, inc=1, device_id={"wide": peer}, device_id_type=MESH)
+
     for load in loads:
         load.start()
-
-    barrier = pltpu.get_barrier_semaphore()
-
-    @pl.loop(1, n)
-    def _(step):
-        pl.semaphore_signal(barrier, inc=1, device_id={"wide": partner(step)}, device_id_type=MESH)
-
     spread = (
         lax.broadcasted_iota(jnp.int32, (vir // BLK, vir), 1) // BLK
         == lax.broadcasted_iota(jnp.int32, (vir // BLK, vir), 0)
@@ -98,23 +100,28 @@
         pltpu.make_async_copy(buffer, buffer, sem).wait()
 
     def exchange(part, received, sems):
-        @pl.loop(1, half)
+        @pl.loop(1, group)
         def _(step):
             peer = neighbour(step)
             pltpu.make_async_remote_copy(
                 src_ref=part.at[peer], dst_ref=received.at[step], send_sem=sems.at[0],
-                recv_sem=sems.at[1], device_id={"wide": side * half + peer},
+                recv_sem=sems.at[1], device_id={"wide": side * group + peer},
                 device_id_type=MESH).start()
 
         received[0] = part[place]
 
-    def across(mid, far, slot):
-        return pltpu.make_async_remote_copy(
-            src_ref=mid.at[1 - side], dst_ref=far, send_sem=far_sem.at[slot],
-            recv_sem=far_sem.at[slot + 1], device_id={"wide": mirror}, device_id_type=MESH)
-
-    occ_across = across(occ_mid, occ_far, 0)
-    aux_across = across(aux_mid, aux_far, 2)
+    def across(mid, far, sems):
+        copies = []
+        for d in range(1, sides):
+            other = lax.rem(side + d, sides)
+            copies.append(pltpu.make_async_remote_copy(
+                src_ref=mid.at[other], dst_ref=far.at[d - 1], send_sem=sems.at[0, d - 1],
+                recv_sem=sems.at[1, d - 1], device_id={"wide": other * group + place},
+                device_id_type=MESH))
+        return copies
+
+    occ_across = across(occ_mid, occ_far, occ_far_sem)
+    aux_across = across(aux_mid, aux_far, aux_far_sem)
 
     for load in loads:
         load.wait()
@@ -136,7 +143,7 @@
 
     total = lax.fori_loop(0, aux, occ_step, jnp.zeros((occ, occ), F32)) * occ_scale
     for d in range(n):
-        occ_part[d % half, d // half] = total[d * own_occ : (d + 1) * own_occ]
+        occ_part[d % group, d // group] = total[d * own_occ : (d + 1) * own_occ]
     exchange(occ_part, occ_recv, occ_sem)
 
     @pl.loop(1, half)
@@ -162,25 +169,29 @@
         g_all[...].reshape(n * aux, depth), c_all[...].reshape(n * aux, depth), NT,
         preferred_element_type=F32,
     )
-    spread_rows = (product * aux_scale).reshape(2, half, aux, n * aux)
-    for h in range(2):
+    spread_rows = (product * aux_scale).reshape(sides, group, aux, n * aux)
+    for h in range(sides):
         aux_part[:, h] = spread_rows[h]
 
     exchange(aux_part, aux_recv, aux_sem)
-    others = pl.ds(1, half - 1)
+    others = pl.ds(1, group - 1)
     take(occ_recv.at[others], occ_sem.at[1])
     occ_mid[...] = jnp.sum(occ_recv[...], axis=0)
-    occ_across.start()
+    for copy in occ_across:
+        copy.start()
     take(send.at[pl.ds(1, n - 1)], send_sem.at[0])
     take(occ_recv.at[others], occ_sem.at[0])
     take(aux_recv.at[others], aux_sem.at[1])
     aux_mid[...] = jnp.sum(aux_recv[...], axis=0)
-    aux_across.start()
+    for copy in aux_across:
+        copy.start()
     take(aux_recv.at[others], aux_sem.at[0])
-    occ_across.wait()
-    occ_ref[...] = occ_mid[side] + occ_far[...]
-    aux_across.wait()
-    aux_ref[...] = aux_mid[side] + aux_far[...]
+    for copy in occ_across:
+        copy.wait()
+    occ_ref[...] = occ_mid[side] + jnp.sum(occ_far[...], axis=0)
+    for copy in aux_across:
+        copy.wait()
+    aux_ref[...] = aux_mid[side] + jnp.sum(aux_far[...], axis=0)
 
 
 def hand_over(occ_in, aux_in, occ_out, aux_out):
@@ -198,7 +209,7 @@
     half = n // 2
     own_occ = occ // n
     density_occ, gamma_aux = pl.pallas_call(
-        functools.partial(kernel, n, occ_scale, aux_scale),
+        functools.partial(kernel, n, SIDES, occ_scale, aux_scale),
         out_shape=(
             jax.ShapeDtypeStruct((occ // n, occ), F32),
             jax.ShapeDtypeStruct((aux, n * aux), F32),
@@ -216,20 +227,21 @@
             pltpu.VMEM((n, 2 * aux, ROWS * width), BF16),
             pltpu.VMEM((half, 2 * aux, ROWS * width), BF16),
             pltpu.VMEM((half, 2 * aux, ROWS * width), BF16),
-            pltpu.VMEM((half, 2, own_occ, occ), F32),
-            pltpu.VMEM((half, 2, own_occ, occ), F32),
-            pltpu.VMEM((2, own_occ, occ), F32),
-            pltpu.VMEM((own_occ, occ), F32),
-            pltpu.VMEM((half, 2, aux, n * aux), F32),
-            pltpu.VMEM((half, 2, aux, n * aux), F32),
-            pltpu.VMEM((2, aux, n * aux), F32),
-            pltpu.VMEM((aux, n * aux), F32),
+            pltpu.VMEM((n // SIDES, SIDES, own_occ, occ), F32),
+            pltpu.VMEM((n // SIDES, SIDES, own_occ, occ), F32),
+            pltpu.VMEM((SIDES, own_occ, occ), F32),
+            pltpu.VMEM((SIDES - 1, own_occ, occ), F32),
+            pltpu.VMEM((n // SIDES, SIDES, aux, n * aux), F32),
+            pltpu.VMEM((n // SIDES, SIDES, aux, n * aux), F32),
+            pltpu.VMEM((SIDES, aux, n * aux), F32),
+            pltpu.VMEM((SIDES - 1, aux, n * aux), F32),
             pltpu.SemaphoreType.DMA((2,)),
             pltpu.SemaphoreType.DMA((1,)),
             pltpu.SemaphoreType.DMA((n,)),
             pltpu.SemaphoreType.DMA((2,)),
             pltpu.SemaphoreType.DMA((2,)),
-            pltpu.SemaphoreType.DMA((4,)),
+            pltpu.SemaphoreType.DMA((2, SIDES - 1)),
+            pltpu.SemaphoreType.DMA((2, SIDES - 1)),
         ],
         compiler_params=pltpu.CompilerParams(
             collective_id=0, has_side_effects=True, vmem_limit_bytes=56 * 1024 * 1024

time: 114 us -> 112 us (0.982)
  Pallas kernels: 113 us -> 111 us
    pallas_call x1, Pallas kernels: 112 us -> 110 us  [local(): pl.pallas_call(functools.partial(kernel, n, SIDES, occ_scale, aux_scale),...]
where the time goes in v5:
time: 112 us
  Pallas kernels  111 us (99%)
    pallas_call x1, Pallas kernels, local(): pl.pallas_call(functools.partial(kernel, n, SIDES, occ_scale, aux_scale),...  110 us

profile of v5, /device:TPU:0, one launch (start us, length us, event | category | flops | bytes accessed | tf_op | source)
XLA Modules:
  0.0 111.8 jit_solution(9768345849880743060)
XLA Ops:
  0.6 109.8 %shard_map.59 = (f32[4,128]{1,0:T(4,128)}, f32[8,256]{1,0:T(8,128)}) custom-call(bf16[8,128,1024]{2,1,0:T(8,128)(2,1)} %g_hbm.1, bf16[8,128,1024]{2,1,0:T(8,128)(2,1)} %c_hbm.1, s32[8,2,16]{2,1,0:T(2,128)} %gb_ref.1, s32[8,2,16]{2,1,0:T(2,128)} %cb_ref.1), custom_call_target="tpu_custom_call" | custom-call | tf_op jit(solution)/shard_map/pallas_call | solution.py:211
  110.5 1.3 %shard_map.60 = (f32[4,128]{1,0:T(4,128)}, f32[8,256]{1,0:T(8,128)}) custom-call(f32[4,128]{1,0:T(4,128)} %get-tuple-element.4.occ_in, f32[8,256]{1,0:T(8,128)} %get-tuple-element.5.aux_in), custom_call_target="tpu_custom_call" | custom-call | tf_op jit(solution)/shard_map/pallas_call | solution.py:254
